TPU v7x, 32 devices: a whole 2x2x4 slice. The times are simulated.
32 devices in a mesh: section: 4 (over y, core), dp: 8 (over z, x).
Axes of the slice: x: 2, y: 2, z: 4, core: 2. Of those that a mesh axis runs over, the one named last changes fastest.
Arguments:
- latents: bfloat16 [6, 176, 1536], P(None, 'dp'), may hold values from -6 to 6
- control_hint: bfloat16 [6, 176, 1536], P(None, 'dp'), may hold values from -6 to 6
- upstream: bfloat16 [6, 176, 1536], P(None, 'dp'), may hold values from -6 to 6
- batch_order: int32 [6], replicated, may hold values from 0 to 5, each once
- section_weight: bfloat16 [4, 1536, 1536], P('section'), may hold values from -0.078125 to 0.078125
- zero_weight: bfloat16 [4, 768, 1536], P('section'), may hold values from -0.0390625 to 0.0390625
Outputs:
- zero_grad: float32 [4, 768, 1536], P('section', 'dp')
Inputs may be any that keep to these rules, and one draw needn't show every extreme that they name: batch_order names each of the 6 micro-batches exactly once.
All inputs are finite; a program needn't handle non-finite values.
Results may differ from a plain program's by a relative error of at most 0.03.
Values may be sent and summed in bfloat16 or wider, within the bound.
A program may use at most 64 MiB of HBM per device.

v0:
```python
import math

import jax
import jax.numpy as jnp
from jax import lax
from jax.sharding import PartitionSpec as P

tanh_coef = 0.7978845608028654
cube_coef = 0.044715


def shifted(value, axis, steps):
    count = lax.axis_size(axis)
    initial, last = (max(0, -steps), min(count, count - steps))
    return lax.ppermute(value, axis, [(source, source + steps) for source in range(initial, last)])


def gelu_value(values):
    inner = tanh_coef * (values + cube_coef * values * values * values)
    return 0.5 * values * (1.0 + jnp.tanh(inner))


def gelu_slope(values):
    inner = tanh_coef * (values + cube_coef * values * values * values)
    tangent = jnp.tanh(inner)
    return 0.5 * (1.0 + tangent) + 0.5 * values * (1.0 - tangent * tangent) * tanh_coef * (
        1.0 + 3.0 * cube_coef * values * values
    )


def keep_row(stored, incoming, active, slot_index):
    previous = lax.dynamic_index_in_dim(stored, slot_index, 0, keepdims=False)
    return lax.dynamic_update_index_in_dim(
        stored, jnp.where(active, incoming, previous), slot_index, 0
    )


def send_down(message):
    return shifted(message, "section", -1)


def body(latents, control_hint, upstream, batch_order, section_weight, zero_weight):
    section_count = lax.axis_size("section")
    block_count = section_count // 2
    section_place = lax.axis_index("section")
    section_depth = section_place // 2
    is_base = section_place % 2 == 0
    weight = section_weight[0]
    zero_rows = zero_weight[0]
    model_width = weight.shape[0]
    half_width = zero_rows.shape[0]
    micro_count = latents.shape[0]
    row_count = latents.shape[1]
    ordered = jnp.take(latents, batch_order, axis=0)
    hinted = jnp.take(control_hint, batch_order, axis=0)
    started = (ordered.astype(jnp.float32) + hinted.astype(jnp.float32)).astype(jnp.bfloat16)
    first_input = jnp.where(is_base, ordered, started)

    def control_work(inputs_now):
        product = jnp.dot(inputs_now, weight, preferred_element_type=jnp.float32)
        control_state = (inputs_now.astype(jnp.float32) + gelu_value(product)).astype(jnp.bfloat16)
        partial_residual = jnp.dot(
            control_state[:, half_width:], zero_rows, preferred_element_type=jnp.float32
        ).astype(jnp.bfloat16)
        message = jnp.concatenate([control_state[:, :half_width], partial_residual], axis=1)
        return (control_state, message, control_state[:, half_width:])

    def control_spare(inputs_now):
        return (
            jnp.zeros_like(inputs_now),
            jnp.zeros((row_count, half_width + model_width), jnp.bfloat16),
            jnp.zeros((row_count, half_width), jnp.bfloat16),
        )

    def base_work(inputs_now, message):
        product = jnp.dot(inputs_now, weight, preferred_element_type=jnp.float32)
        residual_add = jnp.dot(
            message[:, :half_width], zero_rows, preferred_element_type=jnp.float32
        ) + message[:, half_width:].astype(jnp.float32)
        stream_next = (inputs_now.astype(jnp.float32) + gelu_value(product) + residual_add).astype(
            jnp.bfloat16
        )
        return (stream_next, gelu_slope(product), message[:, :half_width])

    def base_spare(inputs_now, message):
        return (
            jnp.zeros_like(inputs_now),
            jnp.zeros((row_count, model_width), jnp.float32),
            jnp.zeros((row_count, half_width), jnp.bfloat16),
        )

    def forward_step(step_index, loop_state):
        chain_in, slopes, side_rows = loop_state
        own_slot = step_index - section_depth
        active = (own_slot >= 0) & (own_slot < micro_count)
        slot_index = jnp.clip(own_slot, 0, micro_count - 1)
        inputs_now = jnp.where(
            section_depth == 0,
            lax.dynamic_index_in_dim(first_input, slot_index, 0, keepdims=False),
            chain_in,
        )
        control_out, message, control_side = lax.cond(
            active & jnp.logical_not(is_base), control_work, control_spare, inputs_now
        )
        received = send_down(message)
        base_out, slope_rows, base_side = lax.cond(
            active & is_base, base_work, base_spare, inputs_now, received
        )
        outgoing = jnp.where(is_base, base_out, control_out)
        slopes = keep_row(slopes, slope_rows, active & is_base, slot_index)
        side_rows = keep_row(
            side_rows, jnp.where(is_base, base_side, control_side), active, slot_index
        )
        chain_in = shifted(outgoing, "section", 2)
        return (chain_in, slopes, side_rows)

    forward_start = (
        jnp.zeros((row_count, model_width), jnp.bfloat16),
        jnp.zeros((micro_count, row_count, model_width), jnp.float32),
        jnp.zeros((micro_count, row_count, half_width), jnp.bfloat16),
    )
    chain_end, slopes, side_rows = lax.fori_loop(
        0, block_count + micro_count - 1, forward_step, forward_start
    )

    def pass_back(grad_in, slope_rows):
        scaled = (grad_in.astype(jnp.float32) * slope_rows).astype(jnp.bfloat16)
        back_term = jnp.dot(scaled, weight.T, preferred_element_type=jnp.float32)
        return (grad_in.astype(jnp.float32) + back_term).astype(jnp.bfloat16)

    def pass_spare(grad_in, slope_rows):
        return jnp.zeros_like(grad_in)

    back_offset = section_count - 1 - section_place

    def backward_step(step_index, loop_state):
        chain_in, grad_rows = loop_state
        own_slot = step_index - back_offset
        active = (own_slot >= 0) & (own_slot < micro_count)
        slot_index = jnp.clip(own_slot, 0, micro_count - 1)
        grad_in = jnp.where(
            section_place == section_count - 1,
            lax.dynamic_index_in_dim(upstream, slot_index, 0, keepdims=False),
            chain_in,
        )
        slope_rows = lax.dynamic_index_in_dim(slopes, slot_index, 0, keepdims=False)
        passed = lax.cond(
            active & is_base & (section_depth > 0), pass_back, pass_spare, grad_in, slope_rows
        )
        outgoing = jnp.where(is_base, passed, grad_in)
        grad_rows = keep_row(grad_rows, grad_in, active, slot_index)
        chain_in = send_down(outgoing)
        return (chain_in, grad_rows)

    backward_start = (
        jnp.zeros((row_count, model_width), jnp.bfloat16),
        jnp.zeros((micro_count, row_count, model_width), jnp.bfloat16),
    )
    back_end, grad_rows = lax.fori_loop(
        0, section_count + micro_count - 1, backward_step, backward_start
    )
    side_flat = side_rows.reshape(-1, half_width)
    grad_flat = grad_rows.reshape(-1, model_width)
    partial_value = jnp.einsum(
        "rs,rd->sd", side_flat, grad_flat, preferred_element_type=jnp.float32
    )
    summed = lax.psum_scatter(
        partial_value[None].astype(jnp.bfloat16), "dp", scatter_dimension=1, tiled=True
    ).astype(jnp.float32)
    grad_scale = 1.0 / math.sqrt(micro_count * row_count * lax.axis_size("dp"))
    return summed * grad_scale


def solution(mesh):
    placed = (
        P(None, "dp", None),
        P(None, "dp", None),
        P(None, "dp", None),
        P(),
        P("section", None, None),
        P("section", None, None),
    )
    return jax.shard_map(
        body, mesh=mesh, in_specs=placed, out_specs=P("section", "dp", None), check_vma=False
    )
```

profile of v0, /device:TPU:0, one launch (start us, length us, event | category | flops | bytes accessed | tf_op | source)
XLA Modules:
  0.0 286.7 jit_solution(5212275108059762036)
XLA Ops:
  8.5 1.6 gather_fusion.1
  10.5 123.3 %while.35 = (s32[]{:T(128)}, bf16[22,1536]{1,0:T(8,128)(2,1)S(1)}, f32[6,22,1536]{2,1,0:T(8,128)S(1)}, bf16[6,22,768]{2,1,0:T(8,128)(2,1)S(1)}, pred[]{:T(512)},...) while((s32[]{:T(128)}, bf16[22,1536]{1,0:T(8,128)(2,1)S(1)}, ...), condition=%wide.region_5.7_spmd, body=%wide.region_0.6_spmd.sunk | while | flops 313218048 | bytes 36385240 | solution.py:122
  13.2 7.1 %collective-permute-done = bf16[22,2304]{1,0:T(8,128)(2,1)S(1)} collective-permute-done((bf16[22,2304]{1,0:T(8,128)(2,1)S(1)}, bf16[22,2304]{1,0:T(8,128)(2,1)S(1)}, u32[]{:S(2)}, u32[]{:S(2)}) %collective-permute-start) | collective-permute-done | bytes 101408 | tf_op jit(solution)/shard_map/while/body/eval_jaxpr/ppermute | solution.py:15
  20.3 5.1 %conditional.7 = (bf16[22,1536]{1,0:T(8,128)(2,1)S(1)}, f32[22,1536]{1,0:T(8,128)S(1)}, bf16[22,768]{1,0:T(8,128)(2,1)}) conditional(s32[]{:T(128)} %convert_element_type.110, () %tuple.96, (bf16[22,1536]{1,0:T(8,128)(2,1)S(1)}, bf16[1536,1536]{1,0:T(8,128)(2,1)}, bf16[22,2304]{1,0:T(8,128)(2,1)S(1)}, bf16[768,1536]{1,0:T(8,128)(2,1)}) %tuple.99), branch_computations={%region_3.4_spmd, %region_4.5_spmd} | conditional | flops 156761088 | bytes 17292340 | solution.py:106
  20.3 3.3 %fusion.12 = (f32[22,1536]{1,0:T(8,128)S(1)}, f32[22,1536]{1,0:T(8,128)S(1)}) fusion(bf16[22,1536]{1,0:T(8,128)(2,1)S(1)} %get-tuple-element.460, bf16[1536,1536]{1,0:T(8,128)(2,1)} %get-tuple-element.461), kind=kOutput, calls=%fused_computation.20 | convolution fusion | flops 104383488 | bytes 5056512 | tf_op jit(solution)/shard_map/while/body/eval_jaxpr/cond/branch_1_fun/dot_general | solution.py:76
  25.4 1.3 collective-permute-start.1
  31.3 5.8 %collective-permute-done = bf16[22,2304]{1,0:T(8,128)(2,1)S(1)} collective-permute-done((bf16[22,2304]{1,0:T(8,128)(2,1)S(1)}, bf16[22,2304]{1,0:T(8,128)(2,1)S(1)}, u32[]{:S(2)}, u32[]{:S(2)}) %collective-permute-start) | collective-permute-done | bytes 101408 | tf_op jit(solution)/shard_map/while/body/eval_jaxpr/ppermute | solution.py:15
  37.1 5.1 %conditional.7 = (bf16[22,1536]{1,0:T(8,128)(2,1)S(1)}, f32[22,1536]{1,0:T(8,128)S(1)}, bf16[22,768]{1,0:T(8,128)(2,1)}) conditional(s32[]{:T(128)} %convert_element_type.110, () %tuple.96, (bf16[22,1536]{1,0:T(8,128)(2,1)S(1)}, bf16[1536,1536]{1,0:T(8,128)(2,1)}, bf16[22,2304]{1,0:T(8,128)(2,1)S(1)}, bf16[768,1536]{1,0:T(8,128)(2,1)}) %tuple.99), branch_computations={%region_3.4_spmd, %region_4.5_spmd} | conditional | flops 156761088 | bytes 17292340 | solution.py:106
  37.1 3.3 %fusion.12 = (f32[22,1536]{1,0:T(8,128)S(1)}, f32[22,1536]{1,0:T(8,128)S(1)}) fusion(bf16[22,1536]{1,0:T(8,128)(2,1)S(1)} %get-tuple-element.460, bf16[1536,1536]{1,0:T(8,128)(2,1)} %get-tuple-element.461), kind=kOutput, calls=%fused_computation.20 | convolution fusion | flops 104383488 | bytes 5056512 | tf_op jit(solution)/shard_map/while/body/eval_jaxpr/cond/branch_1_fun/dot_general | solution.py:76
  42.2 5.0 %collective-permute-start.1 = (bf16[22,1536]{1,0:T(8,128)(2,1)S(1)}, bf16[22,1536]{1,0:T(8,128)(2,1)S(1)}, u32[]{:S(2)}, u32[]{:S(2)}) collective-permute-start(bf16[22,1536]{1,0:T(8,128)(2,1)S(1)} %broadcast_select_fusion.4), channel_id=1, source_target_pairs={{0,16},{8,24},{1,17},{9,25},{2,18},{10,26},{3,19},{11,27},{4,20},{... | collective-permute-start | bytes 202760 | tf_op jit(solution)/shard_map/while/body/eval_jaxpr/ppermute | solution.py:15
  51.9 2.1 collective-permute-done
  54.0 5.1 %conditional.7 = (bf16[22,1536]{1,0:T(8,128)(2,1)S(1)}, f32[22,1536]{1,0:T(8,128)S(1)}, bf16[22,768]{1,0:T(8,128)(2,1)}) conditional(s32[]{:T(128)} %convert_element_type.110, () %tuple.96, (bf16[22,1536]{1,0:T(8,128)(2,1)S(1)}, bf16[1536,1536]{1,0:T(8,128)(2,1)}, bf16[22,2304]{1,0:T(8,128)(2,1)S(1)}, bf16[768,1536]{1,0:T(8,128)(2,1)}) %tuple.99), branch_computations={%region_3.4_spmd, %region_4.5_spmd} | conditional | flops 156761088 | bytes 17292340 | solution.py:106
  54.0 3.3 %fusion.12 = (f32[22,1536]{1,0:T(8,128)S(1)}, f32[22,1536]{1,0:T(8,128)S(1)}) fusion(bf16[22,1536]{1,0:T(8,128)(2,1)S(1)} %get-tuple-element.460, bf16[1536,1536]{1,0:T(8,128)(2,1)} %get-tuple-element.461), kind=kOutput, calls=%fused_computation.20 | convolution fusion | flops 104383488 | bytes 5056512 | tf_op jit(solution)/shard_map/while/body/eval_jaxpr/cond/branch_1_fun/dot_general | solution.py:76
  59.1 5.1 %collective-permute-start.1 = (bf16[22,1536]{1,0:T(8,128)(2,1)S(1)}, bf16[22,1536]{1,0:T(8,128)(2,1)S(1)}, u32[]{:S(2)}, u32[]{:S(2)}) collective-permute-start(bf16[22,1536]{1,0:T(8,128)(2,1)S(1)} %broadcast_select_fusion.4), channel_id=1, source_target_pairs={{0,16},{8,24},{1,17},{9,25},{2,18},{10,26},{3,19},{11,27},{4,20},{... | collective-permute-start | bytes 202760 | tf_op jit(solution)/shard_map/while/body/eval_jaxpr/ppermute | solution.py:15
  68.8 2.1 collective-permute-done
  70.9 5.1 %conditional.7 = (bf16[22,1536]{1,0:T(8,128)(2,1)S(1)}, f32[22,1536]{1,0:T(8,128)S(1)}, bf16[22,768]{1,0:T(8,128)(2,1)}) conditional(s32[]{:T(128)} %convert_element_type.110, () %tuple.96, (bf16[22,1536]{1,0:T(8,128)(2,1)S(1)}, bf16[1536,1536]{1,0:T(8,128)(2,1)}, bf16[22,2304]{1,0:T(8,128)(2,1)S(1)}, bf16[768,1536]{1,0:T(8,128)(2,1)}) %tuple.99), branch_computations={%region_3.4_spmd, %region_4.5_spmd} | conditional | flops 156761088 | bytes 17292340 | solution.py:106
  70.9 3.3 %fusion.12 = (f32[22,1536]{1,0:T(8,128)S(1)}, f32[22,1536]{1,0:T(8,128)S(1)}) fusion(bf16[22,1536]{1,0:T(8,128)(2,1)S(1)} %get-tuple-element.460, bf16[1536,1536]{1,0:T(8,128)(2,1)} %get-tuple-element.461), kind=kOutput, calls=%fused_computation.20 | convolution fusion | flops 104383488 | bytes 5056512 | tf_op jit(solution)/shard_map/while/body/eval_jaxpr/cond/branch_1_fun/dot_general | solution.py:76
  76.0 5.1 %collective-permute-start.1 = (bf16[22,1536]{1,0:T(8,128)(2,1)S(1)}, bf16[22,1536]{1,0:T(8,128)(2,1)S(1)}, u32[]{:S(2)}, u32[]{:S(2)}) collective-permute-start(bf16[22,1536]{1,0:T(8,128)(2,1)S(1)} %broadcast_select_fusion.4), channel_id=1, source_target_pairs={{0,16},{8,24},{1,17},{9,25},{2,18},{10,26},{3,19},{11,27},{4,20},{... | collective-permute-start | bytes 202760 | tf_op jit(solution)/shard_map/while/body/eval_jaxpr/ppermute | solution.py:15
  85.7 2.1 collective-permute-done
  87.8 5.1 %conditional.7 = (bf16[22,1536]{1,0:T(8,128)(2,1)S(1)}, f32[22,1536]{1,0:T(8,128)S(1)}, bf16[22,768]{1,0:T(8,128)(2,1)}) conditional(s32[]{:T(128)} %convert_element_type.110, () %tuple.96, (bf16[22,1536]{1,0:T(8,128)(2,1)S(1)}, bf16[1536,1536]{1,0:T(8,128)(2,1)}, bf16[22,2304]{1,0:T(8,128)(2,1)S(1)}, bf16[768,1536]{1,0:T(8,128)(2,1)}) %tuple.99), branch_computations={%region_3.4_spmd, %region_4.5_spmd} | conditional | flops 156761088 | bytes 17292340 | solution.py:106
  87.8 3.3 %fusion.12 = (f32[22,1536]{1,0:T(8,128)S(1)}, f32[22,1536]{1,0:T(8,128)S(1)}) fusion(bf16[22,1536]{1,0:T(8,128)(2,1)S(1)} %get-tuple-element.460, bf16[1536,1536]{1,0:T(8,128)(2,1)} %get-tuple-element.461), kind=kOutput, calls=%fused_computation.20 | convolution fusion | flops 104383488 | bytes 5056512 | tf_op jit(solution)/shard_map/while/body/eval_jaxpr/cond/branch_1_fun/dot_general | solution.py:76
  92.9 5.1 %collective-permute-start.1 = (bf16[22,1536]{1,0:T(8,128)(2,1)S(1)}, bf16[22,1536]{1,0:T(8,128)(2,1)S(1)}, u32[]{:S(2)}, u32[]{:S(2)}) collective-permute-start(bf16[22,1536]{1,0:T(8,128)(2,1)S(1)} %broadcast_select_fusion.4), channel_id=1, source_target_pairs={{0,16},{8,24},{1,17},{9,25},{2,18},{10,26},{3,19},{11,27},{4,20},{... | collective-permute-start | bytes 202760 | tf_op jit(solution)/shard_map/while/body/eval_jaxpr/ppermute | solution.py:15
  102.6 2.1 collective-permute-done
  104.7 5.1 %conditional.7 = (bf16[22,1536]{1,0:T(8,128)(2,1)S(1)}, f32[22,1536]{1,0:T(8,128)S(1)}, bf16[22,768]{1,0:T(8,128)(2,1)}) conditional(s32[]{:T(128)} %convert_element_type.110, () %tuple.96, (bf16[22,1536]{1,0:T(8,128)(2,1)S(1)}, bf16[1536,1536]{1,0:T(8,128)(2,1)}, bf16[22,2304]{1,0:T(8,128)(2,1)S(1)}, bf16[768,1536]{1,0:T(8,128)(2,1)}) %tuple.99), branch_computations={%region_3.4_spmd, %region_4.5_spmd} | conditional | flops 156761088 | bytes 17292340 | solution.py:106
  104.7 3.3 %fusion.12 = (f32[22,1536]{1,0:T(8,128)S(1)}, f32[22,1536]{1,0:T(8,128)S(1)}) fusion(bf16[22,1536]{1,0:T(8,128)(2,1)S(1)} %get-tuple-element.460, bf16[1536,1536]{1,0:T(8,128)(2,1)} %get-tuple-element.461), kind=kOutput, calls=%fused_computation.20 | convolution fusion | flops 104383488 | bytes 5056512 | tf_op jit(solution)/shard_map/while/body/eval_jaxpr/cond/branch_1_fun/dot_general | solution.py:76
  109.8 5.1 %collective-permute-start.1 = (bf16[22,1536]{1,0:T(8,128)(2,1)S(1)}, bf16[22,1536]{1,0:T(8,128)(2,1)S(1)}, u32[]{:S(2)}, u32[]{:S(2)}) collective-permute-start(bf16[22,1536]{1,0:T(8,128)(2,1)S(1)} %broadcast_select_fusion.4), channel_id=1, source_target_pairs={{0,16},{8,24},{1,17},{9,25},{2,18},{10,26},{3,19},{11,27},{4,20},{... | collective-permute-start | bytes 202760 | tf_op jit(solution)/shard_map/while/body/eval_jaxpr/ppermute | solution.py:15
  119.5 1.9 collective-permute-done
  122.1 9.8 %collective-permute-start.1 = (bf16[22,1536]{1,0:T(8,128)(2,1)S(1)}, bf16[22,1536]{1,0:T(8,128)(2,1)S(1)}, u32[]{:S(2)}, u32[]{:S(2)}) collective-permute-start(bf16[22,1536]{1,0:T(8,128)(2,1)S(1)} %broadcast_select_fusion.4), channel_id=1, source_target_pairs={{0,16},{8,24},{1,17},{9,25},{2,18},{10,26},{3,19},{11,27},{4,20},{... | collective-permute-start | bytes 202760 | tf_op jit(solution)/shard_map/while/body/eval_jaxpr/ppermute | solution.py:15
  133.8 69.0 %while.36 = (s32[]{:T(128)}, bf16[22,1536]{1,0:T(8,128)(2,1)S(1)}, bf16[6,22,1536]{2,1,0:T(8,128)(2,1)S(1)}, pred[]{:T(512)}, s32[]{:T(128)}, /*index=5*/pred[]{...) while((s32[]{:T(128)}, bf16[22,1536]{1,0:T(8,128)(2,1)S(1)}, ...), condition=%wide.region_9.11_spmd, body=%wide.region_6.10_spmd.sunk | while | flops 104113160 | bytes 6052136 | solution.py:159
  134.9 1.3 collective-permute-start.2
  136.2 1.9 collective-permute-done.2
  139.0 1.3 collective-permute-start.2
  140.3 4.6 %collective-permute-done.2 = bf16[22,1536]{1,0:T(8,128)(2,1)S(1)} collective-permute-done((bf16[22,1536]{1,0:T(8,128)(2,1)S(1)}, bf16[22,1536]{1,0:T(8,128)(2,1)S(1)}, u32[]{:S(2)}, u32[]{:S(2)}) %collective-permute-start.2) | collective-permute-done | bytes 67616 | tf_op jit(solution)/shard_map/while/body/eval_jaxpr/ppermute | solution.py:15
  145.9 1.3 collective-permute-start.2
  147.2 6.2 %collective-permute-done.2 = bf16[22,1536]{1,0:T(8,128)(2,1)S(1)} collective-permute-done((bf16[22,1536]{1,0:T(8,128)(2,1)S(1)}, bf16[22,1536]{1,0:T(8,128)(2,1)S(1)}, u32[]{:S(2)}, u32[]{:S(2)}) %collective-permute-start.2) | collective-permute-done | bytes 67616 | tf_op jit(solution)/shard_map/while/body/eval_jaxpr/ppermute | solution.py:15
  154.5 1.3 collective-permute-start.2
  155.8 6.2 %collective-permute-done.2 = bf16[22,1536]{1,0:T(8,128)(2,1)S(1)} collective-permute-done((bf16[22,1536]{1,0:T(8,128)(2,1)S(1)}, bf16[22,1536]{1,0:T(8,128)(2,1)S(1)}, u32[]{:S(2)}, u32[]{:S(2)}) %collective-permute-start.2) | collective-permute-done | bytes 67616 | tf_op jit(solution)/shard_map/while/body/eval_jaxpr/ppermute | solution.py:15
  163.0 1.3 collective-permute-start.2
  164.3 6.2 %collective-permute-done.2 = bf16[22,1536]{1,0:T(8,128)(2,1)S(1)} collective-permute-done((bf16[22,1536]{1,0:T(8,128)(2,1)S(1)}, bf16[22,1536]{1,0:T(8,128)(2,1)S(1)}, u32[]{:S(2)}, u32[]{:S(2)}) %collective-permute-start.2) | collective-permute-done | bytes 67616 | tf_op jit(solution)/shard_map/while/body/eval_jaxpr/ppermute | solution.py:15
  171.6 1.3 collective-permute-start.2
  172.9 6.2 %collective-permute-done.2 = bf16[22,1536]{1,0:T(8,128)(2,1)S(1)} collective-permute-done((bf16[22,1536]{1,0:T(8,128)(2,1)S(1)}, bf16[22,1536]{1,0:T(8,128)(2,1)S(1)}, u32[]{:S(2)}, u32[]{:S(2)}) %collective-permute-start.2) | collective-permute-done | bytes 67616 | tf_op jit(solution)/shard_map/while/body/eval_jaxpr/ppermute | solution.py:15
  180.1 1.3 collective-permute-start.2
  181.4 6.2 %collective-permute-done.2 = bf16[22,1536]{1,0:T(8,128)(2,1)S(1)} collective-permute-done((bf16[22,1536]{1,0:T(8,128)(2,1)S(1)}, bf16[22,1536]{1,0:T(8,128)(2,1)S(1)}, u32[]{:S(2)}, u32[]{:S(2)}) %collective-permute-start.2) | collective-permute-done | bytes 67616 | tf_op jit(solution)/shard_map/while/body/eval_jaxpr/ppermute | solution.py:15
  189.9 6.2 %collective-permute-done.2 = bf16[22,1536]{1,0:T(8,128)(2,1)S(1)} collective-permute-done((bf16[22,1536]{1,0:T(8,128)(2,1)S(1)}, bf16[22,1536]{1,0:T(8,128)(2,1)S(1)}, u32[]{:S(2)}, u32[]{:S(2)}) %collective-permute-start.2) | collective-permute-done | bytes 67616 | tf_op jit(solution)/shard_map/while/body/eval_jaxpr/ppermute | solution.py:15
  198.5 4.4 %collective-permute-done.2 = bf16[22,1536]{1,0:T(8,128)(2,1)S(1)} collective-permute-done((bf16[22,1536]{1,0:T(8,128)(2,1)S(1)}, bf16[22,1536]{1,0:T(8,128)(2,1)S(1)}, u32[]{:S(2)}, u32[]{:S(2)}) %collective-permute-start.2) | collective-permute-done | bytes 67616 | tf_op jit(solution)/shard_map/while/body/eval_jaxpr/ppermute | solution.py:15
  202.8 2.3 fusion.17
  205.1 72.9 %reduce-scatter.2.cloned.1.call-done = bf16[1,96,1536]{2,1,0:T(8,128)(2,1)} async-done(((bf16[1,768,1536]{2,1,0:T(8,128)(2,1)}), bf16[1,96,1536]{2,1,0:T(8,128)(2,1)}) %reduce-scatter.2.cloned.1.call-update) | async-done | bytes 294928 | tf_op jit(solution)/shard_map/reduce_scatter | solution.py:167
  278.0 1.8 convert_multiply_fusion.1
  (173 shorter events, 66.9 us)
Async XLA Ops:
  6.5 1.4 copy-start
  6.5 271.5 %reduce-scatter.2.cloned.1.call-start = ((), (), s32[]{:S(2)}) async-start(), calls=%async_computation.1 | async-start | bytes 2654208 | tf_op jit(solution)/shard_map/reduce_scatter | solution.py:167
  11.9 8.4 %collective-permute-start = (bf16[22,2304]{1,0:T(8,128)(2,1)S(1)}, bf16[22,2304]{1,0:T(8,128)(2,1)S(1)}, u32[]{:S(2)}, u32[]{:S(2)}) collective-permute-start(bf16[22,2304]{1,0:T(8,128)(2,1)S(1)} %get-tuple-element.677), channel_id=1, source_target_pairs={{8,0},{16,8},{24,16},{9,1},{17,9},{25,17},{10,2},{18,10},{26,18},{... | collective-permute-start | bytes 304136 | tf_op jit(solution)/shard_map/while/body/eval_jaxpr/ppermute | solution.py:15
  20.3 3.9 %copy-start.2 = (bf16[768,1536]{1,0:T(8,128)(2,1)S(1)}, bf16[768,1536]{1,0:T(8,128)(2,1)}, u32[]{:S(2)}) copy-start(bf16[768,1536]{1,0:T(8,128)(2,1)} %get-tuple-element.463) | copy-start | bytes 7077892 | tf_op jit(solution)/shard_map/while/body/eval_jaxpr/cond
  25.4 3.3 %collective-permute-start.1 = (bf16[22,1536]{1,0:T(8,128)(2,1)S(1)}, bf16[22,1536]{1,0:T(8,128)(2,1)S(1)}, u32[]{:S(2)}, u32[]{:S(2)}) collective-permute-start(bf16[22,1536]{1,0:T(8,128)(2,1)S(1)} %broadcast_select_fusion.4), channel_id=1, source_target_pairs={{0,16},{8,24},{1,17},{9,25},{2,18},{10,26},{3,19},{11,27},{4,20},{... | collective-permute-start | bytes 202760 | tf_op jit(solution)/shard_map/while/body/eval_jaxpr/ppermute | solution.py:15
  30.0 7.2 %collective-permute-start = (bf16[22,2304]{1,0:T(8,128)(2,1)S(1)}, bf16[22,2304]{1,0:T(8,128)(2,1)S(1)}, u32[]{:S(2)}, u32[]{:S(2)}) collective-permute-start(bf16[22,2304]{1,0:T(8,128)(2,1)S(1)} %get-tuple-element.677), channel_id=1, source_target_pairs={{8,0},{16,8},{24,16},{9,1},{17,9},{25,17},{10,2},{18,10},{26,18},{... | collective-permute-start | bytes 304136 | tf_op jit(solution)/shard_map/while/body/eval_jaxpr/ppermute | solution.py:15
  37.1 3.9 %copy-start.2 = (bf16[768,1536]{1,0:T(8,128)(2,1)S(1)}, bf16[768,1536]{1,0:T(8,128)(2,1)}, u32[]{:S(2)}) copy-start(bf16[768,1536]{1,0:T(8,128)(2,1)} %get-tuple-element.463) | copy-start | bytes 7077892 | tf_op jit(solution)/shard_map/while/body/eval_jaxpr/cond
  42.2 7.0 %collective-permute-start.1 = (bf16[22,1536]{1,0:T(8,128)(2,1)S(1)}, bf16[22,1536]{1,0:T(8,128)(2,1)S(1)}, u32[]{:S(2)}, u32[]{:S(2)}) collective-permute-start(bf16[22,1536]{1,0:T(8,128)(2,1)S(1)} %broadcast_select_fusion.4), channel_id=1, source_target_pairs={{0,16},{8,24},{1,17},{9,25},{2,18},{10,26},{3,19},{11,27},{4,20},{... | collective-permute-start | bytes 202760 | tf_op jit(solution)/shard_map/while/body/eval_jaxpr/ppermute | solution.py:15
  50.6 3.4 %collective-permute-start = (bf16[22,2304]{1,0:T(8,128)(2,1)S(1)}, bf16[22,2304]{1,0:T(8,128)(2,1)S(1)}, u32[]{:S(2)}, u32[]{:S(2)}) collective-permute-start(bf16[22,2304]{1,0:T(8,128)(2,1)S(1)} %get-tuple-element.677), channel_id=1, source_target_pairs={{8,0},{16,8},{24,16},{9,1},{17,9},{25,17},{10,2},{18,10},{26,18},{... | collective-permute-start | bytes 304136 | tf_op jit(solution)/shard_map/while/body/eval_jaxpr/ppermute | solution.py:15
  54.0 3.9 %copy-start.2 = (bf16[768,1536]{1,0:T(8,128)(2,1)S(1)}, bf16[768,1536]{1,0:T(8,128)(2,1)}, u32[]{:S(2)}) copy-start(bf16[768,1536]{1,0:T(8,128)(2,1)} %get-tuple-element.463) | copy-start | bytes 7077892 | tf_op jit(solution)/shard_map/while/body/eval_jaxpr/cond
  59.1 7.1 %collective-permute-start.1 = (bf16[22,1536]{1,0:T(8,128)(2,1)S(1)}, bf16[22,1536]{1,0:T(8,128)(2,1)S(1)}, u32[]{:S(2)}, u32[]{:S(2)}) collective-permute-start(bf16[22,1536]{1,0:T(8,128)(2,1)S(1)} %broadcast_select_fusion.4), channel_id=1, source_target_pairs={{0,16},{8,24},{1,17},{9,25},{2,18},{10,26},{3,19},{11,27},{4,20},{... | collective-permute-start | bytes 202760 | tf_op jit(solution)/shard_map/while/body/eval_jaxpr/ppermute | solution.py:15
  67.5 3.4 %collective-permute-start = (bf16[22,2304]{1,0:T(8,128)(2,1)S(1)}, bf16[22,2304]{1,0:T(8,128)(2,1)S(1)}, u32[]{:S(2)}, u32[]{:S(2)}) collective-permute-start(bf16[22,2304]{1,0:T(8,128)(2,1)S(1)} %get-tuple-element.677), channel_id=1, source_target_pairs={{8,0},{16,8},{24,16},{9,1},{17,9},{25,17},{10,2},{18,10},{26,18},{... | collective-permute-start | bytes 304136 | tf_op jit(solution)/shard_map/while/body/eval_jaxpr/ppermute | solution.py:15
  70.9 3.9 %copy-start.2 = (bf16[768,1536]{1,0:T(8,128)(2,1)S(1)}, bf16[768,1536]{1,0:T(8,128)(2,1)}, u32[]{:S(2)}) copy-start(bf16[768,1536]{1,0:T(8,128)(2,1)} %get-tuple-element.463) | copy-start | bytes 7077892 | tf_op jit(solution)/shard_map/while/body/eval_jaxpr/cond
  76.0 7.1 %collective-permute-start.1 = (bf16[22,1536]{1,0:T(8,128)(2,1)S(1)}, bf16[22,1536]{1,0:T(8,128)(2,1)S(1)}, u32[]{:S(2)}, u32[]{:S(2)}) collective-permute-start(bf16[22,1536]{1,0:T(8,128)(2,1)S(1)} %broadcast_select_fusion.4), channel_id=1, source_target_pairs={{0,16},{8,24},{1,17},{9,25},{2,18},{10,26},{3,19},{11,27},{4,20},{... | collective-permute-start | bytes 202760 | tf_op jit(solution)/shard_map/while/body/eval_jaxpr/ppermute | solution.py:15
  84.4 3.4 %collective-permute-start = (bf16[22,2304]{1,0:T(8,128)(2,1)S(1)}, bf16[22,2304]{1,0:T(8,128)(2,1)S(1)}, u32[]{:S(2)}, u32[]{:S(2)}) collective-permute-start(bf16[22,2304]{1,0:T(8,128)(2,1)S(1)} %get-tuple-element.677), channel_id=1, source_target_pairs={{8,0},{16,8},{24,16},{9,1},{17,9},{25,17},{10,2},{18,10},{26,18},{... | collective-permute-start | bytes 304136 | tf_op jit(solution)/shard_map/while/body/eval_jaxpr/ppermute | solution.py:15
  87.8 3.9 %copy-start.2 = (bf16[768,1536]{1,0:T(8,128)(2,1)S(1)}, bf16[768,1536]{1,0:T(8,128)(2,1)}, u32[]{:S(2)}) copy-start(bf16[768,1536]{1,0:T(8,128)(2,1)} %get-tuple-element.463) | copy-start | bytes 7077892 | tf_op jit(solution)/shard_map/while/body/eval_jaxpr/cond
  92.9 7.1 %collective-permute-start.1 = (bf16[22,1536]{1,0:T(8,128)(2,1)S(1)}, bf16[22,1536]{1,0:T(8,128)(2,1)S(1)}, u32[]{:S(2)}, u32[]{:S(2)}) collective-permute-start(bf16[22,1536]{1,0:T(8,128)(2,1)S(1)} %broadcast_select_fusion.4), channel_id=1, source_target_pairs={{0,16},{8,24},{1,17},{9,25},{2,18},{10,26},{3,19},{11,27},{4,20},{... | collective-permute-start | bytes 202760 | tf_op jit(solution)/shard_map/while/body/eval_jaxpr/ppermute | solution.py:15
  101.3 3.4 %collective-permute-start = (bf16[22,2304]{1,0:T(8,128)(2,1)S(1)}, bf16[22,2304]{1,0:T(8,128)(2,1)S(1)}, u32[]{:S(2)}, u32[]{:S(2)}) collective-permute-start(bf16[22,2304]{1,0:T(8,128)(2,1)S(1)} %get-tuple-element.677), channel_id=1, source_target_pairs={{8,0},{16,8},{24,16},{9,1},{17,9},{25,17},{10,2},{18,10},{26,18},{... | collective-permute-start | bytes 304136 | tf_op jit(solution)/shard_map/while/body/eval_jaxpr/ppermute | solution.py:15
  104.7 3.9 %copy-start.2 = (bf16[768,1536]{1,0:T(8,128)(2,1)S(1)}, bf16[768,1536]{1,0:T(8,128)(2,1)}, u32[]{:S(2)}) copy-start(bf16[768,1536]{1,0:T(8,128)(2,1)} %get-tuple-element.463) | copy-start | bytes 7077892 | tf_op jit(solution)/shard_map/while/body/eval_jaxpr/cond
  109.8 7.1 %collective-permute-start.1 = (bf16[22,1536]{1,0:T(8,128)(2,1)S(1)}, bf16[22,1536]{1,0:T(8,128)(2,1)S(1)}, u32[]{:S(2)}, u32[]{:S(2)}) collective-permute-start(bf16[22,1536]{1,0:T(8,128)(2,1)S(1)} %broadcast_select_fusion.4), channel_id=1, source_target_pairs={{0,16},{8,24},{1,17},{9,25},{2,18},{10,26},{3,19},{11,27},{4,20},{... | collective-permute-start | bytes 202760 | tf_op jit(solution)/shard_map/while/body/eval_jaxpr/ppermute | solution.py:15
  118.2 3.2 %collective-permute-start = (bf16[22,2304]{1,0:T(8,128)(2,1)S(1)}, bf16[22,2304]{1,0:T(8,128)(2,1)S(1)}, u32[]{:S(2)}, u32[]{:S(2)}) collective-permute-start(bf16[22,2304]{1,0:T(8,128)(2,1)S(1)} %get-tuple-element.677), channel_id=1, source_target_pairs={{8,0},{16,8},{24,16},{9,1},{17,9},{25,17},{10,2},{18,10},{26,18},{... | collective-permute-start | bytes 304136 | tf_op jit(solution)/shard_map/while/body/eval_jaxpr/ppermute | solution.py:15
  122.1 11.7 %collective-permute-start.1 = (bf16[22,1536]{1,0:T(8,128)(2,1)S(1)}, bf16[22,1536]{1,0:T(8,128)(2,1)S(1)}, u32[]{:S(2)}, u32[]{:S(2)}) collective-permute-start(bf16[22,1536]{1,0:T(8,128)(2,1)S(1)} %broadcast_select_fusion.4), channel_id=1, source_target_pairs={{0,16},{8,24},{1,17},{9,25},{2,18},{10,26},{3,19},{11,27},{4,20},{... | collective-permute-start | bytes 202760 | tf_op jit(solution)/shard_map/while/body/eval_jaxpr/ppermute | solution.py:15
  134.9 3.2 %collective-permute-start.2 = (bf16[22,1536]{1,0:T(8,128)(2,1)S(1)}, bf16[22,1536]{1,0:T(8,128)(2,1)S(1)}, u32[]{:S(2)}, u32[]{:S(2)}) collective-permute-start(bf16[22,1536]{1,0:T(8,128)(2,1)S(1)} %broadcast_select_fusion.5), channel_id=1, source_target_pairs={{8,0},{16,8},{24,16},{9,1},{17,9},{25,17},{10,2},{18,10},{26,18},{... | collective-permute-start | bytes 202760 | tf_op jit(solution)/shard_map/while/body/eval_jaxpr/ppermute | solution.py:15
  139.0 5.9 %collective-permute-start.2 = (bf16[22,1536]{1,0:T(8,128)(2,1)S(1)}, bf16[22,1536]{1,0:T(8,128)(2,1)S(1)}, u32[]{:S(2)}, u32[]{:S(2)}) collective-permute-start(bf16[22,1536]{1,0:T(8,128)(2,1)S(1)} %broadcast_select_fusion.5), channel_id=1, source_target_pairs={{8,0},{16,8},{24,16},{9,1},{17,9},{25,17},{10,2},{18,10},{26,18},{... | collective-permute-start | bytes 202760 | tf_op jit(solution)/shard_map/while/body/eval_jaxpr/ppermute | solution.py:15
  145.9 7.5 %collective-permute-start.2 = (bf16[22,1536]{1,0:T(8,128)(2,1)S(1)}, bf16[22,1536]{1,0:T(8,128)(2,1)S(1)}, u32[]{:S(2)}, u32[]{:S(2)}) collective-permute-start(bf16[22,1536]{1,0:T(8,128)(2,1)S(1)} %broadcast_select_fusion.5), channel_id=1, source_target_pairs={{8,0},{16,8},{24,16},{9,1},{17,9},{25,17},{10,2},{18,10},{26,18},{... | collective-permute-start | bytes 202760 | tf_op jit(solution)/shard_map/while/body/eval_jaxpr/ppermute | solution.py:15
  154.5 7.5 %collective-permute-start.2 = (bf16[22,1536]{1,0:T(8,128)(2,1)S(1)}, bf16[22,1536]{1,0:T(8,128)(2,1)S(1)}, u32[]{:S(2)}, u32[]{:S(2)}) collective-permute-start(bf16[22,1536]{1,0:T(8,128)(2,1)S(1)} %broadcast_select_fusion.5), channel_id=1, source_target_pairs={{8,0},{16,8},{24,16},{9,1},{17,9},{25,17},{10,2},{18,10},{26,18},{... | collective-permute-start | bytes 202760 | tf_op jit(solution)/shard_map/while/body/eval_jaxpr/ppermute | solution.py:15
  163.0 7.5 %collective-permute-start.2 = (bf16[22,1536]{1,0:T(8,128)(2,1)S(1)}, bf16[22,1536]{1,0:T(8,128)(2,1)S(1)}, u32[]{:S(2)}, u32[]{:S(2)}) collective-permute-start(bf16[22,1536]{1,0:T(8,128)(2,1)S(1)} %broadcast_select_fusion.5), channel_id=1, source_target_pairs={{8,0},{16,8},{24,16},{9,1},{17,9},{25,17},{10,2},{18,10},{26,18},{... | collective-permute-start | bytes 202760 | tf_op jit(solution)/shard_map/while/body/eval_jaxpr/ppermute | solution.py:15
  171.6 7.5 %collective-permute-start.2 = (bf16[22,1536]{1,0:T(8,128)(2,1)S(1)}, bf16[22,1536]{1,0:T(8,128)(2,1)S(1)}, u32[]{:S(2)}, u32[]{:S(2)}) collective-permute-start(bf16[22,1536]{1,0:T(8,128)(2,1)S(1)} %broadcast_select_fusion.5), channel_id=1, source_target_pairs={{8,0},{16,8},{24,16},{9,1},{17,9},{25,17},{10,2},{18,10},{26,18},{... | collective-permute-start | bytes 202760 | tf_op jit(solution)/shard_map/while/body/eval_jaxpr/ppermute | solution.py:15
  180.1 7.5 %collective-permute-start.2 = (bf16[22,1536]{1,0:T(8,128)(2,1)S(1)}, bf16[22,1536]{1,0:T(8,128)(2,1)S(1)}, u32[]{:S(2)}, u32[]{:S(2)}) collective-permute-start(bf16[22,1536]{1,0:T(8,128)(2,1)S(1)} %broadcast_select_fusion.5), channel_id=1, source_target_pairs={{8,0},{16,8},{24,16},{9,1},{17,9},{25,17},{10,2},{18,10},{26,18},{... | collective-permute-start | bytes 202760 | tf_op jit(solution)/shard_map/while/body/eval_jaxpr/ppermute | solution.py:15
  188.6 7.5 %collective-permute-start.2 = (bf16[22,1536]{1,0:T(8,128)(2,1)S(1)}, bf16[22,1536]{1,0:T(8,128)(2,1)S(1)}, u32[]{:S(2)}, u32[]{:S(2)}) collective-permute-start(bf16[22,1536]{1,0:T(8,128)(2,1)S(1)} %broadcast_select_fusion.5), channel_id=1, source_target_pairs={{8,0},{16,8},{24,16},{9,1},{17,9},{25,17},{10,2},{18,10},{26,18},{... | collective-permute-start | bytes 202760 | tf_op jit(solution)/shard_map/while/body/eval_jaxpr/ppermute | solution.py:15
  197.2 5.7 %collective-permute-start.2 = (bf16[22,1536]{1,0:T(8,128)(2,1)S(1)}, bf16[22,1536]{1,0:T(8,128)(2,1)S(1)}, u32[]{:S(2)}, u32[]{:S(2)}) collective-permute-start(bf16[22,1536]{1,0:T(8,128)(2,1)S(1)} %broadcast_select_fusion.5), channel_id=1, source_target_pairs={{8,0},{16,8},{24,16},{9,1},{17,9},{25,17},{10,2},{18,10},{26,18},{... | collective-permute-start | bytes 202760 | tf_op jit(solution)/shard_map/while/body/eval_jaxpr/ppermute | solution.py:15
Sparse Core Ops, SparseCore 0:
  205.2 72.7 reduce-scatter.1
where the time goes:
time: 289 us; the launch traced here: 287 us
  waiting for transfers between devices  152 us (53%)
  starting transfers between devices  57.1 us (20%)
  matrix products  29.1 us (10%)
  other arithmetic  17.9 us (6%)
  local copies, waits for them, and re-layouts  15.9 us (6%)
  between operations  13.5 us (5%)
    ppermute x23, waiting for transfers between devices, shifted(): lax.ppermute(value, axis, [(source, source + steps) for source in range(i...  79.2 us
    reduce_scatter x1, waiting for transfers between devices, body(): lax.psum_scatter(partial_value[None].astype(jnp.bfloat16), 'dp', scatter_...  72.9 us
    ppermute x23, starting transfers between devices, shifted(): lax.ppermute(value, axis, [(source, source + steps) for source in range(i...  57.1 us
    dot_general x6, matrix products, base_work(): product = jnp.dot(inputs_now, weight, preferred_element_type=jnp.float32)  19.6 us
    dynamic_update_slice x23, other arithmetic, keep_row(): lax.dynamic_update_index_in_dim(stored, jnp.where(active, incoming, previ...  14.1 us
    another operation x35, local copies, waits for them, and re-layouts  9.61 us
    dot_general x6, matrix products, base_work(): jnp.dot(message[:, :half_width], zero_rows, preferred_element_type=jnp.fl...  7.17 us
  transfers between devices with their start and end apart: 24, of which 24 were waited for; matrix products, arithmetic and copies ran while one was open for 2% of the time, Pallas kernels for 0%

commit v1 on v0

v1 whole, which is shorter than its diff:
```python
import functools
import math

import jax
import jax.numpy as jnp
from jax import lax
from jax.experimental import pallas as pl
from jax.experimental.pallas import tpu as pltpu
from jax.sharding import PartitionSpec as P

tanh_coef = 0.7978845608028654
cube_coef = 0.044715
f32 = jnp.float32
bf16 = jnp.bfloat16


def gelu_parts(values):
    square = values * values
    tangent = jnp.tanh(tanh_coef * (values + cube_coef * square * values))
    return square, tangent


def gelu_value(values):
    _, tangent = gelu_parts(values)
    return 0.5 * values * (1.0 + tangent)


def gelu_slope(values):
    square, tangent = gelu_parts(values)
    return 0.5 * (1.0 + tangent) + 0.5 * values * (1.0 - tangent * tangent) * tanh_coef * (
        1.0 + 3.0 * cube_coef * square
    )


def mm(left, right):
    return jnp.dot(left, right, preferred_element_type=f32)


def kernel(
    blocks, n_dp, order_ref, lat_ref, hint_ref, up_ref, w_hbm, z_hbm, out_ref,
    w, z, flat, chain, mine, side, resid, pout, back, slope, gbuf, et, ecol,
    load_sem, chain_s, chain_r, side_s, side_r, resid_s, resid_r, back_s, back_r,
    e_s, e_r, ag_s, ag_r, sib_s, sib_r,
):
    sections = 2 * blocks
    line = n_dp // 2
    micro, rows, width = lat_ref.shape
    half = width // 2
    padded = flat.shape[0]
    share = et.shape[1]
    place = lax.axis_index("section")
    me = lax.axis_index("dp")
    depth = place // 2
    parity = place % 2
    sibling = place + 1 - 2 * parity
    here, across = me // 2, me % 2
    partner = me + 1 - 2 * across
    is_base = parity == 0
    is_control = parity == 1
    last = depth == blocks - 1

    load_w = pltpu.make_async_copy(w_hbm.at[0], w, load_sem.at[0])
    load_z = pltpu.make_async_copy(z_hbm.at[0], z, load_sem.at[1])
    load_w.start()
    load_z.start()

    barrier = pltpu.get_barrier_semaphore()

    def greet(step, carry):
        pl.semaphore_signal(
            barrier, inc=1, device_id={"dp": lax.rem(me + step, n_dp)},
            device_id_type=pl.DeviceIdType.MESH,
        )
        return carry

    lax.fori_loop(1, n_dp, greet, 0)
    greeted = n_dp - 1
    for step in (-2, -1, 1, 2):
        there = place + step
        inside = (there >= 0) & (there < sections)

        @pl.when(inside)
        def _():
            pl.semaphore_signal(
                barrier, inc=1, device_id={"section": there}, device_id_type=pl.DeviceIdType.MESH
            )

        greeted = greeted + jnp.where(inside, 1, 0)

    def remote(src, dst, send, recv, **where):
        return pltpu.make_async_remote_copy(
            src_ref=src, dst_ref=dst, send_sem=send, recv_sem=recv, device_id=where,
            device_id_type=pl.DeviceIdType.MESH,
        )

    def fill(slot_rows, target):
        flat[padded - 16 :, :] = jnp.zeros((16, width), f32)
        for slot in range(micro):
            flat[slot * rows : (slot + 1) * rows, :] = slot_rows(slot)
        for part in range(2):
            target[part] = flat[:, part * half : (part + 1) * half].astype(bf16)

    @pl.when((depth == 0) & is_base)
    def _():
        fill(lambda slot: lat_ref[order_ref[slot]].astype(f32), chain)

    @pl.when((depth == 0) & is_control)
    def _():
        fill(
            lambda slot: lat_ref[order_ref[slot]].astype(f32) + hint_ref[order_ref[slot]].astype(f32),
            chain,
        )

    @pl.when(last)
    def _():
        fill(lambda slot: up_ref[slot].astype(f32), gbuf.at[me])

    out_ref[...] = jnp.zeros_like(out_ref)
    pl.semaphore_wait(barrier, greeted)

    def go_up(d):
        return remote(gbuf.at[d, parity], gbuf.at[d, parity], ag_s.at[0, d], ag_r.at[d], dp=me + 2)

    def go_down(d):
        return remote(gbuf.at[d, parity], gbuf.at[d, parity], ag_s.at[1, d], ag_r.at[d], dp=me - 2)

    def go_across(d):
        return remote(gbuf.at[d, parity], gbuf.at[d, parity], ag_s.at[2, d], ag_r.at[d], dp=partner)

    def go_sibling(d):
        return remote(gbuf.at[d, parity], gbuf.at[d, parity], sib_s.at[d], sib_r.at[d], section=sibling)

    def arrived(d):
        return remote(gbuf.at[d, parity], gbuf.at[d, parity], ag_s.at[2, d], ag_r.at[d], dp=partner)

    def arrived_sibling(d):
        return remote(
            gbuf.at[d, 1 - parity], gbuf.at[d, 1 - parity], sib_s.at[d], sib_r.at[d], section=sibling
        )

    def gather_start():
        @pl.when(here + 1 < line)
        def _():
            go_up(me).start()

        @pl.when(here > 0)
        def _():
            go_down(me).start()

        go_across(me).start()

    @pl.when(last)
    def _():
        gather_start()

    load_w.wait()
    load_z.wait()

    def product(source, part):
        return sum(
            mm(source[inner], w[inner * half : (inner + 1) * half, part * half : (part + 1) * half])
            for inner in range(2)
        )

    def to_chain(part):
        return remote(mine.at[part], chain.at[part], chain_s.at[part], chain_r.at[part], section=place + 2)

    def from_chain(part):
        return remote(mine.at[part], chain.at[part], chain_s.at[part], chain_r.at[part], section=sibling)

    to_side = remote(mine.at[0], side, side_s, side_r, section=place - 1)
    from_side = remote(mine.at[0], side, side_s, side_r, section=sibling)

    def to_resid(part):
        return remote(pout.at[part], resid.at[part], resid_s.at[part], resid_r.at[part], section=place - 1)

    def from_resid(part):
        return remote(pout.at[part], resid.at[part], resid_s.at[part], resid_r.at[part], section=sibling)

    def to_back(part):
        return remote(back.at[part], gbuf.at[me, part], back_s.at[part], back_r, section=place - 2 + part)

    from_back = remote(back.at[0], gbuf.at[me, parity], back_s.at[0], back_r, section=sibling)

    def spread(columns):
        turned = columns.astype(f32).T
        for d in range(n_dp):
            et[d] = turned[d * share : (d + 1) * share, :].astype(bf16)
        ecol[me] = et[me]

        def send(step, carry):
            there = lax.rem(me + step, n_dp)
            remote(et.at[there], ecol.at[me], e_s.at[step], e_r.at[me], dp=there).start()
            return carry

        lax.fori_loop(1, n_dp, send, 0)

    @pl.when(depth > 0)
    def _():
        from_chain(0).wait_recv()
        from_chain(1).wait_recv()

    @pl.when(is_control)
    def _():
        for part in range(2):
            value = product(chain, part)
            mine[part] = (chain[part].astype(f32) + gelu_value(value)).astype(bf16)
            if part == 0:
                to_side.start()

            @pl.when(jnp.logical_not(last))
            def _():
                to_chain(part).start()

        @pl.when(jnp.logical_not(last))
        def _():
            for part in range(2):
                pout[part] = mm(mine[1], z[:, part * half : (part + 1) * half]).astype(bf16)
                to_resid(part).start()

        spread(mine[1])

        @pl.when(jnp.logical_not(last))
        def _():
            from_back.wait_recv()
            gather_start()
            go_sibling(me).start()

    @pl.when(is_base)
    def _():
        for part in range(2):
            value = product(chain, part)

            @pl.when(depth > 0)
            def _():
                slope[:, part * half : (part + 1) * half] = gelu_slope(value)

            @pl.when(jnp.logical_not(last))
            def _():
                base = chain[part].astype(f32) + gelu_value(value)
                if part == 0:
                    from_side.wait_recv()
                added = mm(side[...], z[:, part * half : (part + 1) * half])
                from_resid(part).wait_recv()
                mine[part] = (base + added + resid[part].astype(f32)).astype(bf16)
                to_chain(part).start()

        @pl.when((depth == 0) & jnp.logical_not(last))
        def _():
            spread(side[...])

        @pl.when(jnp.logical_not(last))
        def _():
            from_back.wait_recv()
            gather_start()
            go_sibling(me).start()

        @pl.when(depth > 0)
        def _():
            @pl.when(jnp.logical_not(last))
            def _():
                arrived_sibling(me).wait_recv()

            scaled = [
                (gbuf[me, part].astype(f32) * slope[:, part * half : (part + 1) * half]).astype(bf16)
                for part in range(2)
            ]
            for part in range(2):
                term = sum(
                    lax.dot_general(
                        scaled[inner],
                        w[part * half : (part + 1) * half, inner * half : (inner + 1) * half],
                        (((1,), (1,)), ((), ())),
                        preferred_element_type=f32,
                    )
                    for inner in range(2)
                )
                back[part] = (gbuf[me, part].astype(f32) + term).astype(bf16)
                to_back(part).start()

        @pl.when((depth > 0) | last)
        def _():
            @pl.when(last)
            def _():
                from_side.wait_recv()

            spread(side[...])

    def add_chunk(d):
        @pl.when(d != me)
        def _():
            remote(et.at[d], ecol.at[d], e_s.at[0], e_r.at[d], dp=partner).wait_recv()

        for part in range(2):
            cut = slice(part * half, (part + 1) * half)
            out_ref[:, cut] += mm(ecol[d], gbuf[d, part])

    def gather_step(reach, carry):
        @pl.when(here - reach >= 0)
        def _():
            d = me - 2 * reach
            arrived(d).wait_recv()

            @pl.when(here + 1 < line)
            def _():
                go_up(d).start()

            go_across(d).start()
            go_sibling(d).start()

        @pl.when(here + reach < line)
        def _():
            d = me + 2 * reach
            arrived(d).wait_recv()

            @pl.when(here > 0)
            def _():
                go_down(d).start()

            go_across(d).start()
            go_sibling(d).start()

        near = reach - 1

        def crossed(shift):
            d = partner + shift
            arrived(d).wait_recv()
            go_sibling(d).start()

        def finish(shift):
            @pl.when(jnp.logical_not((shift == 0) & last) & ((shift != 0) | is_control | (depth == 0)))
            def _():
                arrived_sibling(me + shift).wait_recv()

            add_chunk(me + shift)
            arrived_sibling(partner + shift).wait_recv()
            add_chunk(partner + shift)

        low = here - near >= 0
        high = (here + near < line) & (near > 0)
        for job in (crossed, finish):

            @pl.when(low)
            def _():
                job(-2 * near)

            @pl.when(high)
            def _():
                job(2 * near)

        return carry

    lax.fori_loop(1, line + 1, gather_step, 0)

    @pl.when(is_control)
    def _():
        to_side.wait_send()

        @pl.when(jnp.logical_not(last))
        def _():
            for part in range(2):
                to_resid(part).wait_send()

    @pl.when(jnp.logical_not(last))
    def _():
        for part in range(2):
            to_chain(part).wait_send()

    @pl.when(is_base & (depth > 0))
    def _():
        for part in range(2):
            to_back(part).wait_send()

    def drain(d, carry):
        @pl.when(d > 0)
        def _():
            remote(et.at[d], ecol.at[d], e_s.at[d], e_r.at[d], dp=partner).wait_send()

        @pl.when(d % 2 == across)
        def _():
            @pl.when((d <= me) & (here + 1 < line))
            def _():
                go_up(d).wait_send()

            @pl.when((d >= me) & (here > 0))
            def _():
                go_down(d).wait_send()

            go_across(d).wait_send()

        @pl.when((d != me) | jnp.logical_not(last))
        def _():
            go_sibling(d).wait_send()

        return carry

    lax.fori_loop(0, n_dp, drain, 0)


def body(blocks, n_dp, latents, control_hint, upstream, batch_order, section_weight, zero_weight):
    micro, rows, width = latents.shape
    half = zero_weight.shape[1]
    share = half // n_dp
    padded = (micro * rows + 15) // 16 * 16
    vmem = pl.BlockSpec(memory_space=pltpu.VMEM)
    whole = pl.BlockSpec(memory_space=pl.ANY)
    dma = pltpu.SemaphoreType.DMA
    summed = pl.pallas_call(
        functools.partial(kernel, blocks, n_dp),
        out_shape=jax.ShapeDtypeStruct((share, width), f32),
        in_specs=[pl.BlockSpec(memory_space=pltpu.SMEM), vmem, vmem, vmem, whole, whole],
        out_specs=vmem,
        scratch_shapes=[
            pltpu.VMEM((width, width), bf16),
            pltpu.VMEM((half, width), bf16),
            pltpu.VMEM((padded, width), f32),
            pltpu.VMEM((2, padded, half), bf16),
            pltpu.VMEM((2, padded, half), bf16),
            pltpu.VMEM((padded, half), bf16),
            pltpu.VMEM((2, padded, half), bf16),
            pltpu.VMEM((2, padded, half), bf16),
            pltpu.VMEM((2, padded, half), bf16),
            pltpu.VMEM((padded, width), f32),
            pltpu.VMEM((n_dp, 2, padded, half), bf16),
            pltpu.VMEM((n_dp, share, padded), bf16),
            pltpu.VMEM((n_dp, share, padded), bf16),
            dma((2,)), dma((2,)), dma((2,)), dma, dma, dma((2,)), dma((2,)), dma((2,)), dma,
            dma((n_dp,)), dma((n_dp,)), dma((3, n_dp)), dma((n_dp,)), dma((n_dp,)), dma((n_dp,)),
        ],
        compiler_params=pltpu.CompilerParams(
            collective_id=0, has_side_effects=True, vmem_limit_bytes=50 * 1024 * 1024
        ),
    )(batch_order, latents, control_hint, upstream, section_weight, zero_weight)
    grad_scale = 1.0 / math.sqrt(micro * rows * n_dp)
    return summed[None] * grad_scale


def solution(mesh):
    placed = (
        P(None, "dp", None),
        P(None, "dp", None),
        P(None, "dp", None),
        P(),
        P("section", None, None),
        P("section", None, None),
    )
    return jax.shard_map(
        functools.partial(body, mesh.shape["section"] // 2, mesh.shape["dp"]),
        mesh=mesh, in_specs=placed, out_specs=P("section", "dp", None), check_vma=False,
    )
```

time: 289 us -> 58.7 us (0.20)
  waiting for transfers between devices: 152 us -> 0 us
  starting transfers between devices: 57.1 us -> 0 us
  Pallas kernels: 0 us -> 53.8 us
  matrix products: 29.1 us -> 0 us
  other arithmetic: 17.9 us -> 0.87 us
  between operations: 13.5 us -> 0.01 us
  local copies, waits for them, and re-layouts: 15.9 us -> 3.69 us
    ppermute x23 -> x0, waiting for transfers between devices: 79.2 us -> none  [shifted(): lax.ppermute(value, axis, [(source, source + steps) for source in range(i...]
    reduce_scatter x1 -> x0, waiting for transfers between devices: 72.9 us -> none  [body(): lax.psum_scatter(partial_value[None].astype(jnp.bfloat16), 'dp', scatter_...]
    ppermute x23 -> x0, starting transfers between devices: 57.1 us -> none  [shifted(): lax.ppermute(value, axis, [(source, source + steps) for source in range(i...]
    pallas_call x0 -> x1, Pallas kernels: none -> 53.8 us  [body(): pl.pallas_call(functools.partial(kernel, blocks, n_dp), out_shape=jax.Sha...]
    dot_general x13 -> x0, matrix products: 29.1 us -> none  [the longest x6 19.6 us: base_work(): product = jnp.dot(inputs_now, weight, preferred_element_type=jnp.float32)]
    dynamic_update_slice x23 -> x0, other arithmetic: 14.1 us -> none  [keep_row(): lax.dynamic_update_index_in_dim(stored, jnp.where(active, incoming, previ...]
    another operation x35 -> x0, local copies, waits for them, and re-layouts: 9.61 us -> none
    unnamed x2 -> x8, local copies, waits for them, and re-layouts: 0.01 us -> 3.69 us
  transfers between devices with their start and end apart: 24 -> 0, of which waited for: 24 -> 0; matrix products, arithmetic and copies ran while one was open for 2% -> 0% of each run, Pallas kernels for 0% -> 0%
where the time goes in v1:
time: 58.7 us; the launch traced here: 58.3 us
  Pallas kernels  53.8 us (92%)
  local copies, waits for them, and re-layouts  3.69 us (6%)
  other arithmetic  0.87 us (1%)
    pallas_call x1, Pallas kernels, body(): pl.pallas_call(functools.partial(kernel, blocks, n_dp), out_shape=jax.Sha...  53.8 us
    unnamed x8, local copies, waits for them, and re-layouts  3.69 us

profile of v1, /device:TPU:0, one launch (start us, length us, event | category | flops | bytes accessed | tf_op | source)
XLA Modules:
  0.0 58.3 jit_solution(3588609450082779577)
XLA Ops:
  0.0 0.0 copy-start
  0.0 1.0 %copy-done = bf16[6,22,1536]{2,1,0:T(8,128)(2,1)S(1)} copy-done((bf16[6,22,1536]{2,1,0:T(8,128)(2,1)S(1)}, bf16[6,22,1536]{2,1,0:T(8,128)(2,1)}, u32[]{:S(2)}) %copy-start) | copy-done | bytes 405528
  1.0 0.0 copy-start.1
  1.0 1.0 %copy-done.1 = bf16[6,22,1536]{2,1,0:T(8,128)(2,1)S(1)} copy-done((bf16[6,22,1536]{2,1,0:T(8,128)(2,1)S(1)}, bf16[6,22,1536]{2,1,0:T(8,128)(2,1)}, u32[]{:S(2)}) %copy-start.1) | copy-done | bytes 405528
  2.0 0.0 copy-start.2
  2.0 1.0 %copy-done.2 = bf16[6,22,1536]{2,1,0:T(8,128)(2,1)S(1)} copy-done((bf16[6,22,1536]{2,1,0:T(8,128)(2,1)S(1)}, bf16[6,22,1536]{2,1,0:T(8,128)(2,1)}, u32[]{:S(2)}) %copy-start.2) | copy-done | bytes 405528
  3.0 0.0 copy-start.3
  3.0 0.7 %copy-done.3 = s32[6]{0:T(128)S(1)} copy-done((s32[6]{0:T(128)S(1)}, s32[6]{0:T(128)}, u32[]{:S(2)}) %copy-start.3) | copy-done | bytes 48
  3.7 53.8 %shard_map.64 = f32[96,1536]{1,0:T(8,128)S(1)} custom-call(s32[6]{0:T(128)S(1)} %copy-done.3, bf16[6,22,1536]{2,1,0:T(8,128)(2,1)S(1)} %copy-done, bf16[6,22,1536]{2,1,0:T(8,128)(2,1)S(1)} %copy-done.1, bf16[6,22,1536]{2,1,0:T(8,128)(2,1)S(1)} %copy-done.2, bf16[1,1536,1536]{2,1,0:T(8,128)(2,1)} %w_hbm.1, bf16[1,768,1536]{2,1,0:T(8,128)(2,1)} %z_hbm.1), custom_call_target="tpu_custom_call" | custom-call | tf_op jit(solution)/shard_map/pallas_call | solution.py:408
  57.5 0.9 %multiply_bitcast_fusion = f32[1,96,1536]{2,1,0:T(8,128)} fusion(f32[96,1536]{1,0:T(8,128)S(1)} %shard_map.64), kind=kLoop, calls=%fused_computation | loop fusion | flops 147456 | bytes 1179648 | tf_op jit(solution)/shard_map/mul | solution.py:435
Async XLA Ops:
  0.0 1.0 %copy-start = (bf16[6,22,1536]{2,1,0:T(8,128)(2,1)S(1)}, bf16[6,22,1536]{2,1,0:T(8,128)(2,1)}, u32[]{:S(2)}) copy-start(bf16[6,22,1536]{2,1,0:T(8,128)(2,1)} %lat_ref.1) | copy-start | bytes 1216516
  1.0 1.0 %copy-start.1 = (bf16[6,22,1536]{2,1,0:T(8,128)(2,1)S(1)}, bf16[6,22,1536]{2,1,0:T(8,128)(2,1)}, u32[]{:S(2)}) copy-start(bf16[6,22,1536]{2,1,0:T(8,128)(2,1)} %hint_ref.1) | copy-start | bytes 1216516
  2.0 1.0 %copy-start.2 = (bf16[6,22,1536]{2,1,0:T(8,128)(2,1)S(1)}, bf16[6,22,1536]{2,1,0:T(8,128)(2,1)}, u32[]{:S(2)}) copy-start(bf16[6,22,1536]{2,1,0:T(8,128)(2,1)} %up_ref.1) | copy-start | bytes 1216516
  3.0 0.7 %copy-start.3 = (s32[6]{0:T(128)S(1)}, s32[6]{0:T(128)}, u32[]{:S(2)}) copy-start(s32[6]{0:T(128)} %order_ref.1) | copy-start | bytes 76
